TPU v7x, 512 devices: a whole 4x8x8 slice. The times are simulated.
512 devices in a mesh: section: 4 (over x), ctx: 128 (over z, y, core).
Axes of the slice: x: 4, y: 8, z: 8, core: 2. Of those that a mesh axis runs over, the one named last changes fastest.
Arguments:
- gate_values: bfloat16 [4, 16384, 4096], P('section', 'ctx'), may hold values from -6 to 6
- conv_input: bfloat16 [4, 16384, 4096], P('section', 'ctx'), may hold values from -6 to 6
- sent_grads: bfloat16 [4, 16384, 4096], P('section', 'ctx'), may hold values from -6 to 6
- filter_taps: float32 [4, 256, 128], P('section'), may hold values from -0.5 to 0.5
- doc_lengths: int32 [4, 128], P('section'), may hold values from 1 to 512, 16384 in all within a row
Outputs:
- input_grad: bfloat16 [4, 16384, 4096], P('section', 'ctx')
- filter_grad: float32 [4, 256, 128], P('section')
Inputs may be any that keep to these rules, and one draw needn't show every extreme that they name: `doc_lengths`: each row sums to 16384; its largest length is exactly 512.
All inputs are finite; a program needn't handle non-finite values.
Results may differ from a plain program's by a relative error of at most 0.011.
Values may be sent and summed in bfloat16 or wider, within the bound.
No kernel may reach another device: no remote copies, remote signals or barrier semaphores. Data moves between devices by JAX's collectives and lax.ppermute only.
A program may use at most 64 MiB of HBM per device.

v0:
```python
import jax
import jax.numpy as jnp
from jax import lax
from jax.sharding import PartitionSpec as P


def passed_along(value, axis, steps):
    count = lax.axis_size(axis)
    pairs = [(source, (source + steps) % count) for source in range(count)]
    return lax.ppermute(value, axis, pairs)


def passed_along_2(value, axis, steps):
    count = lax.axis_size(axis)
    first, last = (max(0, -steps), min(count, count - steps))
    return lax.ppermute(value, axis, [(source, source + steps) for source in range(first, last)])


def on_device(gate_values, conv_input, sent_grads, filter_taps, doc_lengths):
    tok_rows = gate_values.shape[1]
    channels = gate_values.shape[2]
    group_count = filter_taps.shape[1]
    tap_count = filter_taps.shape[2]
    members = channels // group_count
    lag_block = 16
    turns = tap_count // lag_block
    arrived = passed_along(sent_grads, "section", -1)
    scaled = (arrived[0].astype(jnp.float32) * gate_values[0].astype(jnp.float32)).astype(
        jnp.bfloat16
    )
    ahead = passed_along_2(scaled[: tap_count - 1], "ctx", -1)
    extended = jnp.concatenate([scaled, ahead, jnp.zeros((1, channels), jnp.bfloat16)], axis=0)
    doc_bounds = jnp.cumsum(doc_lengths[0])
    total_tokens = doc_bounds[-1]
    positions = lax.axis_index("ctx") * tok_rows + jnp.arange(tok_rows, dtype=jnp.int32)
    doc_end = jnp.min(
        jnp.where(doc_bounds[None, :] > positions[:, None], doc_bounds[None, :], total_tokens),
        axis=1,
    )
    lags = jnp.arange(tap_count, dtype=jnp.int32)
    inside = (positions[:, None] + lags[None, :] < doc_end[:, None]).astype(jnp.float32)
    own_rows = conv_input[0]
    taps_channel = jnp.repeat(
        filter_taps[0].astype(jnp.bfloat16).astype(jnp.float32), members, axis=0
    )
    behind = passed_along_2(own_rows[tok_rows - (tap_count - 1) :], "ctx", 1)
    past_ext = jnp.concatenate([jnp.zeros((1, channels), jnp.bfloat16), behind, own_rows], axis=0)
    doc_begin = jnp.max(
        jnp.where(doc_bounds[None, :] <= positions[:, None], doc_bounds[None, :], 0), axis=1
    )
    reach = (positions[:, None] - lags[None, :] >= doc_begin[:, None]).astype(jnp.float32)
    fixed_rows = scaled.astype(jnp.float32)

    def one_turn(turn, carried):
        grad_rows, grad_taps = carried
        first = turn * lag_block
        window = lax.dynamic_slice_in_dim(extended, first, tok_rows + lag_block, 0).astype(
            jnp.float32
        )
        back_start = tap_count - first - lag_block + 1
        back_window = lax.dynamic_slice_in_dim(
            past_ext, back_start, tok_rows + lag_block - 1, 0
        ).astype(jnp.float32)
        columns = []
        for step in range(lag_block):
            offset = first + step
            mask_col = lax.dynamic_slice_in_dim(inside, offset, 1, 1)
            tap_col = lax.dynamic_slice_in_dim(taps_channel, offset, 1, 1)[:, 0]
            term = window[step : step + tok_rows] * mask_col
            grad_rows = grad_rows + term * tap_col[None, :]
            reach_col = lax.dynamic_slice_in_dim(reach, offset, 1, 1)
            partner = back_window[lag_block - 1 - step : lag_block - 1 - step + tok_rows]
            product = fixed_rows * partner * reach_col
            columns.append(jnp.sum(product, axis=0).reshape(group_count, members).sum(axis=1))
        block_cols = jnp.stack(columns, axis=1)
        grad_taps = lax.dynamic_update_slice(grad_taps, block_cols, (0, first))
        return (grad_rows, grad_taps)

    start = (
        jnp.zeros((tok_rows, channels), jnp.float32),
        jnp.zeros((group_count, tap_count), jnp.float32),
    )
    grad_rows, local_taps = lax.fori_loop(0, turns, one_turn, start)
    filter_grad = lax.psum(local_taps, "ctx")
    return (grad_rows.astype(jnp.bfloat16)[None], filter_grad[None])


def solution(mesh):
    return jax.shard_map(
        on_device,
        mesh=mesh,
        in_specs=(
            P("section", "ctx", None),
            P("section", "ctx", None),
            P("section", "ctx", None),
            P("section", None, None),
            P("section", None),
        ),
        out_specs=(P("section", "ctx", None), P("section", None, None)),
        check_vma=False,
    )
```

profile of v0, /device:TPU:1, one launch (start us, length us, event | category | flops | bytes accessed | tf_op | source)
XLA Modules:
  0.0 439.3 jit_solution(16008284839260995243)
XLA Ops:
  7.2 5.3 %collective-permute-start = (bf16[1,128,4096]{2,1,0:T(8,128)(2,1)}, bf16[1,128,4096]{2,1,0:T(8,128)(2,1)S(1)}, u32[]{:S(2)}, u32[]{:S(2)}) collective-permute-start(bf16[1,128,4096]{2,1,0:T(8,128)(2,1)} %param.9), channel_id=1, source_target_pairs={{0,384},{128,0},{256,128},{384,256},{1,385},{129,1},{257,129},{385... | collective-permute-start | bytes 3145736 | tf_op jit(solution)/shard_map/ppermute | solution.py:10
  15.0 4.0 collective-permute-start.2
  19.1 12.9 %collective-permute-done = bf16[1,128,4096]{2,1,0:T(8,128)(2,1)S(1)} collective-permute-done((bf16[1,128,4096]{2,1,0:T(8,128)(2,1)}, bf16[1,128,4096]{2,1,0:T(8,128)(2,1)S(1)}, u32[]{:S(2)}, u32[]{:S(2)}) %collective-permute-start) | collective-permute-done | bytes 1048608 | tf_op jit(solution)/shard_map/ppermute | solution.py:10
  33.4 6.1 %collective-permute-start.1 = (bf16[127,4096]{1,0:T(8,128)(2,1)}, bf16[127,4096]{1,0:T(8,128)(2,1)}, u32[]{:S(2)}, u32[]{:S(2)}) collective-permute-start(bf16[127,4096]{1,0:T(8,128)(2,1)} %slice_bitcast_fusion), channel_id=1, source_target_pairs={{1,0},{2,1},{3,2},{4,3},{5,4},{6,5},{7,6},{8,7},{9,8},{10,9},{11,1... | collective-permute-start | bytes 3121160 | tf_op jit(solution)/shard_map/ppermute | solution.py:16
  41.9 2.9 copy.12
  45.6 7.9 %collective-permute-done.1 = bf16[127,4096]{1,0:T(8,128)(2,1)} collective-permute-done((bf16[127,4096]{1,0:T(8,128)(2,1)}, bf16[127,4096]{1,0:T(8,128)(2,1)}, u32[]{:S(2)}, u32[]{:S(2)}) %collective-permute-start.1) | collective-permute-done | bytes 1040416 | tf_op jit(solution)/shard_map/ppermute | solution.py:16
  53.5 3.8 pad_maximum_fusion.1
  57.4 186.1 %while.20 = (s32[]{:T(128)}, f32[128,4096]{1,0:T(8,128)}, f32[256,128]{0,1:T(8,128)S(1)}, bf16[256,4096]{1,0:T(8,128)(2,1)}, f32[128,128]{0,1:T(8,128)S(1)}, /*i...) while((s32[]{:T(128)}, f32[128,4096]{1,0:T(8,128)}, ...), condition=%wide.region_36.37_spmd.clone, body=%wide.region_3.36_spmd.clone.sunk | while | flops 52027460 | bytes 101295480 | solution.py:83
  61.6 2.9 fusion.104
  64.6 3.5 fusion.105
  73.6 5.8 %fusion.103 = f32[128,4096]{1,0:T(8,128)S(1)} fusion(f32[144,4096]{1,0:T(8,128)S(1)} %dynamic-slice_convert_fusion.4, f32[128,4096]{1,0:T(8,128)S(1)} %copy-done, f32[4096]{0:T(1024)S(1)} %bitcast.182, f32[128]{0:T(128)S(1)} %get-tuple-element.572, f32[4096]{0:T(1024)S(1)} %bitcast.183, f32[128]{0:T(128)S(1)} %get-tuple-element.574, ...), kind=kLoop, calls=%fused_computation.50.clone.1 | loop fusion | flops 25690112 | bytes 38019072 | tf_op jit(solution)/shard_map/while/body/eval_jaxpr/add | solution.py:70
  84.9 2.9 fusion.104
  87.8 3.5 fusion.105
  96.8 5.8 %fusion.103 = f32[128,4096]{1,0:T(8,128)S(1)} fusion(f32[144,4096]{1,0:T(8,128)S(1)} %dynamic-slice_convert_fusion.4, f32[128,4096]{1,0:T(8,128)S(1)} %copy-done, f32[4096]{0:T(1024)S(1)} %bitcast.182, f32[128]{0:T(128)S(1)} %get-tuple-element.572, f32[4096]{0:T(1024)S(1)} %bitcast.183, f32[128]{0:T(128)S(1)} %get-tuple-element.574, ...), kind=kLoop, calls=%fused_computation.50.clone.1 | loop fusion | flops 25690112 | bytes 38019072 | tf_op jit(solution)/shard_map/while/body/eval_jaxpr/add | solution.py:70
  108.1 2.9 fusion.104
  111.1 3.5 fusion.105
  120.1 5.8 %fusion.103 = f32[128,4096]{1,0:T(8,128)S(1)} fusion(f32[144,4096]{1,0:T(8,128)S(1)} %dynamic-slice_convert_fusion.4, f32[128,4096]{1,0:T(8,128)S(1)} %copy-done, f32[4096]{0:T(1024)S(1)} %bitcast.182, f32[128]{0:T(128)S(1)} %get-tuple-element.572, f32[4096]{0:T(1024)S(1)} %bitcast.183, f32[128]{0:T(128)S(1)} %get-tuple-element.574, ...), kind=kLoop, calls=%fused_computation.50.clone.1 | loop fusion | flops 25690112 | bytes 38019072 | tf_op jit(solution)/shard_map/while/body/eval_jaxpr/add | solution.py:70
  131.4 2.9 fusion.104
  134.3 3.5 fusion.105
  143.3 5.8 %fusion.103 = f32[128,4096]{1,0:T(8,128)S(1)} fusion(f32[144,4096]{1,0:T(8,128)S(1)} %dynamic-slice_convert_fusion.4, f32[128,4096]{1,0:T(8,128)S(1)} %copy-done, f32[4096]{0:T(1024)S(1)} %bitcast.182, f32[128]{0:T(128)S(1)} %get-tuple-element.572, f32[4096]{0:T(1024)S(1)} %bitcast.183, f32[128]{0:T(128)S(1)} %get-tuple-element.574, ...), kind=kLoop, calls=%fused_computation.50.clone.1 | loop fusion | flops 25690112 | bytes 38019072 | tf_op jit(solution)/shard_map/while/body/eval_jaxpr/add | solution.py:70
  154.6 2.9 fusion.104
  157.5 3.5 fusion.105
  166.5 5.8 %fusion.103 = f32[128,4096]{1,0:T(8,128)S(1)} fusion(f32[144,4096]{1,0:T(8,128)S(1)} %dynamic-slice_convert_fusion.4, f32[128,4096]{1,0:T(8,128)S(1)} %copy-done, f32[4096]{0:T(1024)S(1)} %bitcast.182, f32[128]{0:T(128)S(1)} %get-tuple-element.572, f32[4096]{0:T(1024)S(1)} %bitcast.183, f32[128]{0:T(128)S(1)} %get-tuple-element.574, ...), kind=kLoop, calls=%fused_computation.50.clone.1 | loop fusion | flops 25690112 | bytes 38019072 | tf_op jit(solution)/shard_map/while/body/eval_jaxpr/add | solution.py:70
  177.8 2.9 fusion.104
  180.7 3.5 fusion.105
  189.8 5.8 %fusion.103 = f32[128,4096]{1,0:T(8,128)S(1)} fusion(f32[144,4096]{1,0:T(8,128)S(1)} %dynamic-slice_convert_fusion.4, f32[128,4096]{1,0:T(8,128)S(1)} %copy-done, f32[4096]{0:T(1024)S(1)} %bitcast.182, f32[128]{0:T(128)S(1)} %get-tuple-element.572, f32[4096]{0:T(1024)S(1)} %bitcast.183, f32[128]{0:T(128)S(1)} %get-tuple-element.574, ...), kind=kLoop, calls=%fused_computation.50.clone.1 | loop fusion | flops 25690112 | bytes 38019072 | tf_op jit(solution)/shard_map/while/body/eval_jaxpr/add | solution.py:70
  201.0 2.9 fusion.104
  204.0 3.5 fusion.105
  213.0 5.8 %fusion.103 = f32[128,4096]{1,0:T(8,128)S(1)} fusion(f32[144,4096]{1,0:T(8,128)S(1)} %dynamic-slice_convert_fusion.4, f32[128,4096]{1,0:T(8,128)S(1)} %copy-done, f32[4096]{0:T(1024)S(1)} %bitcast.182, f32[128]{0:T(128)S(1)} %get-tuple-element.572, f32[4096]{0:T(1024)S(1)} %bitcast.183, f32[128]{0:T(128)S(1)} %get-tuple-element.574, ...), kind=kLoop, calls=%fused_computation.50.clone.1 | loop fusion | flops 25690112 | bytes 38019072 | tf_op jit(solution)/shard_map/while/body/eval_jaxpr/add | solution.py:70
  227.2 3.5 fusion.105
  236.3 5.8 %fusion.103 = f32[128,4096]{1,0:T(8,128)S(1)} fusion(f32[144,4096]{1,0:T(8,128)S(1)} %dynamic-slice_convert_fusion.4, f32[128,4096]{1,0:T(8,128)S(1)} %copy-done, f32[4096]{0:T(1024)S(1)} %bitcast.182, f32[128]{0:T(128)S(1)} %get-tuple-element.572, f32[4096]{0:T(1024)S(1)} %bitcast.183, f32[128]{0:T(128)S(1)} %get-tuple-element.574, ...), kind=kLoop, calls=%fused_computation.50.clone.1 | loop fusion | flops 25690112 | bytes 38019072 | tf_op jit(solution)/shard_map/while/body/eval_jaxpr/add | solution.py:70
  246.9 183.9 %all-reduce.2.cloned.1.call-done = f32[1,256,128]{2,1,0:T(8,128)} async-done(((f32[1,256,128]{2,1,0:T(8,128)}), f32[1,256,128]{2,1,0:T(8,128)}) %all-reduce.2.cloned.1.call-update) | async-done | bytes 131088 | tf_op jit(solution)/shard_map/psum | solution.py:84
  (364 shorter events, 100.5 us)
Async XLA Ops:
  7.2 423.7 %all-reduce.2.cloned.1.call-start = ((), (), s32[]{:S(2)}) async-start(), calls=%async_computation | async-start | bytes 262144 | tf_op jit(solution)/shard_map/psum | solution.py:84
  7.2 24.8 %copy-start.2 = (bf16[1,128,4096]{2,1,0:T(8,128)(2,1)S(1)}, bf16[1,128,4096]{2,1,0:T(8,128)(2,1)}, u32[]{:S(2)}) copy-start(bf16[1,128,4096]{2,1,0:T(8,128)(2,1)} %param.7) | copy-start | bytes 3145732
  7.2 24.8 %collective-permute-start = (bf16[1,128,4096]{2,1,0:T(8,128)(2,1)}, bf16[1,128,4096]{2,1,0:T(8,128)(2,1)S(1)}, u32[]{:S(2)}, u32[]{:S(2)}) collective-permute-start(bf16[1,128,4096]{2,1,0:T(8,128)(2,1)} %param.9), channel_id=1, source_target_pairs={{0,384},{128,0},{256,128},{384,256},{1,385},{129,1},{257,129},{385... | collective-permute-start | bytes 3145736 | tf_op jit(solution)/shard_map/ppermute | solution.py:10
  15.0 30.6 %collective-permute-start.2 = (bf16[127,4096]{1,0:T(8,128)(2,1)}, bf16[127,4096]{1,0:T(8,128)(2,1)}, u32[]{:S(2)}, u32[]{:S(2)}) collective-permute-start(bf16[127,4096]{1,0:T(8,128)(2,1)} %slice_bitcast_fusion.1), channel_id=1, source_target_pairs={{0,1},{1,2},{2,3},{3,4},{4,5},{5,6},{6,7},{7,8},{8,9},{9,10},{10,1... | collective-permute-start | bytes 3121160 | tf_op jit(solution)/shard_map/ppermute | solution.py:16
  32.3 7.2 %copy-start.4 = (s32[1,128]{1,0:T(1,128)S(1)}, s32[1,128]{1,0:T(1,128)}, u32[]{:S(2)}) copy-start(s32[1,128]{1,0:T(1,128)} %param.11) | copy-start | bytes 1540
  32.3 8.1 %copy-start.3 = (f32[1,256,128]{2,1,0:T(8,128)S(1)}, f32[1,256,128]{2,1,0:T(8,128)}, u32[]{:S(2)}) copy-start(f32[1,256,128]{2,1,0:T(8,128)} %param.10) | copy-start | bytes 393220
  33.4 20.1 %collective-permute-start.1 = (bf16[127,4096]{1,0:T(8,128)(2,1)}, bf16[127,4096]{1,0:T(8,128)(2,1)}, u32[]{:S(2)}, u32[]{:S(2)}) collective-permute-start(bf16[127,4096]{1,0:T(8,128)(2,1)} %slice_bitcast_fusion), channel_id=1, source_target_pairs={{1,0},{2,1},{3,2},{4,3},{5,4},{6,5},{7,6},{8,7},{9,8},{10,9},{11,1... | collective-permute-start | bytes 3121160 | tf_op jit(solution)/shard_map/ppermute | solution.py:16
  71.6 2.0 copy-start
  79.4 1.3 copy-start.1
  94.9 2.0 copy-start
  102.7 1.3 copy-start.1
  118.1 2.0 copy-start
  125.9 1.3 copy-start.1
  141.4 2.0 copy-start
  149.2 1.3 copy-start.1
  164.6 2.0 copy-start
  172.4 1.3 copy-start.1
  187.8 2.0 copy-start
  195.6 1.3 copy-start.1
  211.1 2.0 copy-start
  218.9 1.3 copy-start.1
  234.3 2.0 copy-start
  242.1 1.3 copy-start.1
Sparse Core Ops, SparseCore 0:
  244.4 186.4 all-reduce.1
where the time goes:
time: 440 us; the launch traced here: 439 us
  waiting for transfers between devices  205 us (47%)
  other arithmetic  146 us (33%)
  local copies, waits for them, and re-layouts  56.6 us (13%)
  starting transfers between devices  15.5 us (4%)
  between operations  14.2 us (3%)
    psum x1, waiting for transfers between devices, on_device(): filter_grad = lax.psum(local_taps, 'ctx')  184 us
    reduce_sum x144, other arithmetic, one_turn(): jnp.sum(product, axis=0).reshape(group_count, members).sum(axis=1)  65.1 us
    add x8, other arithmetic, one_turn(): grad_rows = grad_rows + term * tap_col[None, :]  46.7 us
    dynamic_slice x8, local copies, waits for them, and re-layouts, one_turn(): tap_col = lax.dynamic_slice_in_dim(taps_channel, offset, 1, 1)[:, 0]  19.3 us
    convert_element_type x8, other arithmetic, one_turn(): lax.dynamic_slice_in_dim(extended, first, tok_rows + lag_block, 0)  13.3 us
    ppermute x1, waiting for transfers between devices, passed_along(): return lax.ppermute(value, axis, pairs)  12.9 us
    convert_element_type x8, other arithmetic, one_turn(): back_window = lax.dynamic_slice_in_dim(past_ext, back_start, tok_rows + l...  12.9 us
    while x32, local copies, waits for them, and re-layouts  12.7 us
  transfers between devices with their start and end apart: 4, of which 3 were waited for; matrix products, arithmetic and copies ran while one was open for 3% of the time, Pallas kernels for 0%

commit v1 on v0

v1 whole, which is shorter than its diff:
```python
import functools
import jax
import jax.numpy as jnp
from jax import lax
from jax.experimental import pallas as pl
from jax.experimental.pallas import tpu as pltpu
from jax.sharding import PartitionSpec as P

BF, F32 = jnp.bfloat16, jnp.float32
TOK, CH, GRP, TAPS, FILT = 128, 4096, 16, 128, 256
VMEM = pl.BlockSpec(memory_space=pltpu.VMEM)
ROOM = 16 * 1024 * 1024


def lag_sums(products, flip):
    hi = products.astype(BF)
    lo = (products - hi.astype(F32)).astype(BF)
    flipped = jnp.dot(hi, flip, preferred_element_type=F32) + jnp.dot(lo, flip, preferred_element_type=F32)
    rows = []
    for g in range(products.shape[0] // 8):
        one = pltpu.roll(flipped[8 * g : 8 * g + 8], 0, 1, stride=1, stride_axis=0)
        rows.append(jnp.sum(one, axis=0, keepdims=True))
    return jnp.concatenate(rows, axis=0)


def taps_kernel(start, arr_ref, gate_ref, beh_ref, own_ref, mask_ref, *rest):
    acc_ref = rest[-1]
    width = arr_ref.shape[1]
    mask = mask_ref[...]
    row = lax.broadcasted_iota(jnp.int32, (TOK, TOK), 0)
    lane = lax.broadcasted_iota(jnp.int32, (TOK, TOK), 1)
    tri = lane <= row
    flip = ((row + lane) % TAPS == 0).astype(F32).astype(BF)
    chosen = (lane[:8] // GRP == row[:8]).astype(F32).astype(BF)
    s_ref, g_ref = rest[-3:-1]
    for h in range(width // 128):
        here = slice(128 * h, 128 * h + 128)
        there = slice(start + 128 * h, start + 128 * h + 128)
        s = (arr_ref[:, here].astype(F32) * gate_ref[:, there].astype(F32)).astype(BF)
        s_ref[:, here] = s
        past = jnp.concatenate([beh_ref[:, here], own_ref[:, there]], axis=0)
        for g in range(8):
            one = s * chosen[g : g + 1, :]
            prod = lax.dot_general(one, past, (((1,), (1,)), ((), ())), preferred_element_type=F32)
            both = jnp.where(tri, prod[:, 128:], prod[:, :128]) * mask
            part = both[0:8]
            for a in range(1, 16):
                part = part + pltpu.roll(both[8 * a : 8 * a + 8], 128 - 8 * a, 1)
            acc_ref[64 * h + 8 * g : 64 * h + 8 * g + 8, :] = part
    sums = lag_sums(acc_ref[...], flip)
    if len(g_ref.shape) == 2:
        g_ref[...] = sums
    else:
        whole = jnp.concatenate([r[...] for r in rest[:-3]] + [sums], axis=0)
        n, per = g_ref.shape[:2]
        for i in range(n):
            g_ref[i] = whole[per * i : per * i + per].astype(BF)


def taps_block(arr, gate, behind, own, mask, start, before=(), parts=None):
    width = arr.shape[1]
    if parts:
        sums = jax.ShapeDtypeStruct((parts, FILT // parts, TAPS), BF)
    else:
        sums = jax.ShapeDtypeStruct((width // GRP, TAPS), F32)
    args = (arr, gate, *behind, own, mask, *before)
    return pl.pallas_call(
        functools.partial(taps_kernel, start),
        in_specs=[VMEM] * len(args),
        out_specs=[VMEM, VMEM],
        out_shape=[jax.ShapeDtypeStruct((TOK, width), BF), sums],
        scratch_shapes=[pltpu.VMEM((width // 2, 128), F32)],
        compiler_params=pltpu.CompilerParams(vmem_limit_bytes=ROOM),
        cost_estimate=pl.CostEstimate(flops=1 << 56, bytes_accessed=width << 11, transcendentals=0),
        name=f"taps_block_{start}",
    )(*args)


def rows_kernel(start, offset, width, s_ref, ahead_ref, taps_ref, mask_ref, *rest):
    o_ref, block, sem = rest[-3:]
    mask = mask_ref[...]
    lane = lax.broadcasted_iota(jnp.int32, (TOK, 128), 1) // GRP
    for h in range(width // 128):
        here = slice(128 * h, 128 * h + 128)
        there = slice(offset + 128 * h, offset + 128 * h + 128)
        ext = jnp.concatenate([s_ref[:, there], ahead_ref[:, there]], axis=0)
        acc = None
        for g in range(8):
            f = (start + 128 * h) // GRP + g
            base = jnp.broadcast_to(taps_ref[f : f + 1, :], (8, 128))
            base = pltpu.roll(base, 0, 1, stride=1, stride_axis=0)
            circ = jnp.concatenate([base] + [pltpu.roll(base, 8 * a, 1) for a in range(1, 16)], axis=0).astype(BF)
            toep = jnp.concatenate([circ, circ], axis=1) * mask
            prod = jnp.dot(toep, ext, preferred_element_type=F32)
            acc = prod if acc is None else jnp.where(lane == g, prod, acc)
        block[:, here] = acc.astype(BF)
    copy = pltpu.make_async_copy(block, o_ref.at[:, pl.ds(start, width)], sem)
    copy.start()
    copy.wait()


def rows_block(scaled, ahead, taps, mask, out, start, offset, width):
    specs = [VMEM] * 4
    args = [scaled, ahead, taps, mask]
    if out is not None:
        specs.append(pl.BlockSpec(memory_space=pl.ANY))
        args.append(out)
    return pl.pallas_call(
        functools.partial(rows_kernel, start, offset, width),
        in_specs=specs,
        out_specs=pl.BlockSpec(memory_space=pl.ANY),
        out_shape=jax.ShapeDtypeStruct((TOK, CH), BF),
        input_output_aliases={4: 0} if out is not None else {},
        scratch_shapes=[pltpu.VMEM((TOK, width), BF), pltpu.SemaphoreType.DMA(())],
        compiler_params=pltpu.CompilerParams(vmem_limit_bytes=ROOM),
        cost_estimate=pl.CostEstimate(flops=width << 18, bytes_accessed=width << 10, transcendentals=0),
        name=f"rows_block_{start}",
    )(*args)


def sum_kernel(parts_ref, o_ref):
    total = parts_ref[0].astype(F32)
    for i in range(1, parts_ref.shape[0]):
        total = total + parts_ref[i].astype(F32)
    total = total.astype(BF)
    for i in range(o_ref.shape[0]):
        o_ref[i] = total


def summed(parts, copies):
    return pl.pallas_call(
        sum_kernel,
        in_specs=[VMEM],
        out_specs=VMEM,
        out_shape=jax.ShapeDtypeStruct((copies,) + parts.shape[1:], BF),
        compiler_params=pltpu.CompilerParams(vmem_limit_bytes=ROOM),
        cost_estimate=pl.CostEstimate(flops=1 << 56, bytes_accessed=parts.size * 2, transcendentals=0),
        name=f"sum_of_{parts.shape[0]}",
    )(parts)


def cut_kernel(whole_ref, *rest):
    n = len(rest) // 2
    copies, at = [], 0
    for i in range(n):
        width = rest[i].shape[1]
        copies.append(pltpu.make_async_copy(whole_ref.at[:, pl.ds(at, width)], rest[i], rest[n + i]))
        at += width
    for copy in copies:
        copy.start()
    for copy in copies:
        copy.wait()


def cut(whole, widths):
    return pl.pallas_call(
        cut_kernel,
        in_specs=[pl.BlockSpec(memory_space=pltpu.HBM)],
        out_specs=[VMEM] * len(widths),
        out_shape=[jax.ShapeDtypeStruct((TOK, w), BF) for w in widths],
        scratch_shapes=[pltpu.SemaphoreType.DMA(()) for _ in widths],
        compiler_params=pltpu.CompilerParams(vmem_limit_bytes=56 * 1024 * 1024),
        name="cut",
    )(whole)


def mask_kernel(base_ref, len_ref, ahead_ref, behind_ref):
    row = lax.broadcasted_iota(jnp.int32, (128, 128), 0)
    col = lax.broadcasted_iota(jnp.int32, (128, 128), 1)
    upto = (row <= col).astype(F32).astype(BF)
    lengths = jnp.broadcast_to(len_ref[...], (8, 128))
    high = lengths // 16
    low = lengths - 16 * high
    bounds = 16.0 * jnp.dot(high.astype(F32).astype(BF), upto, preferred_element_type=F32)
    bounds = bounds + jnp.dot(low.astype(F32).astype(BF), upto, preferred_element_type=F32)
    bounds = jnp.broadcast_to(bounds[0:1, :], (TOK, 128))
    base = base_ref[0, 0]
    here = (base + row).astype(F32)
    ended = bounds <= here
    end = jnp.min(jnp.where(ended, 2.0 * CH * TAPS, bounds), axis=1, keepdims=True)
    begin = jnp.max(jnp.where(ended, bounds, 0.0), axis=1, keepdims=True)
    source = base + jnp.where(col <= row, col, col - TOK)
    behind_ref[...] = (source.astype(F32) >= begin).astype(F32)
    own = (base + col).astype(F32)
    ahead_ref[:, :TOK] = jnp.where((col >= row) & (own < end), 1.0, 0.0).astype(BF)
    ahead_ref[:, TOK:] = jnp.where((col < row) & (own + 1.0 * TOK < end), 1.0, 0.0).astype(BF)


def masks(doc_lengths, base):
    return pl.pallas_call(
        mask_kernel,
        in_specs=[pl.BlockSpec(memory_space=pltpu.SMEM), VMEM],
        out_specs=[VMEM, VMEM],
        out_shape=[jax.ShapeDtypeStruct((TOK, 2 * TOK), BF), jax.ShapeDtypeStruct((TOK, TOK), F32)],
        compiler_params=pltpu.CompilerParams(vmem_limit_bytes=ROOM),
        name="masks",
    )(base.reshape(1, 1), doc_lengths.reshape(1, 128))


def last_sum_kernel(rows, parts_ref, o_ref):
    sets = FILT // rows
    for r in range(sets):
        total = parts_ref[r].astype(F32)
        for i in range(r + sets, parts_ref.shape[0], sets):
            total = total + parts_ref[i].astype(F32)
        o_ref[rows * r : rows * r + rows, :] = total


def last_sum(parts):
    return pl.pallas_call(
        functools.partial(last_sum_kernel, parts.shape[1]),
        in_specs=[VMEM],
        out_specs=VMEM,
        out_shape=jax.ShapeDtypeStruct((FILT, TAPS), F32),
        compiler_params=pltpu.CompilerParams(vmem_limit_bytes=ROOM),
        name="last_sum",
    )(parts)


WIDTHS = (2048, 2048)


def place(z, y, c):
    return (z * 8 + y) * 2 + c


PLANES = [[place(z + i, y, c) for i in range(2) for y in range(8) for c in range(2)] for z in range(0, 8, 2)]


def shifted(value, axis, steps):
    count = lax.axis_size(axis)
    return lax.ppermute(value, axis, [(i, (i + steps) % count) for i in range(count)])


def exchanged(value, groups):
    return lax.all_to_all(value, "ctx", 0, 0, axis_index_groups=groups)


def tied(value, *after):
    return lax.optimization_barrier((value, *after))[0]


def on_device(gate_values, conv_input, sent_grads, filter_taps, doc_lengths):
    gate, conv, sent, taps = gate_values[0], conv_input[0], sent_grads[0], filter_taps[0]
    base = lax.axis_index("ctx") * TOK
    w0, w1 = WIDTHS
    piece0, piece1 = cut(sent, WIDTHS)
    arr0 = shifted(piece0, "section", -1)
    arr1 = shifted(piece1, "section", -1)
    behind = [shifted(piece, "ctx", 1) for piece in cut(tied(conv, piece0), (CH // 2, CH // 2))]
    ahead_mask, behind_mask = masks(tied(doc_lengths, arr0), base)
    s0, g0 = taps_block(arr0, gate, behind[:1], conv, behind_mask, 0)
    ahead0 = shifted(s0, "ctx", -1)
    s1, local = taps_block(arr1, gate, behind[1:], conv, behind_mask, w0, (g0,), 32)
    got = exchanged(local, PLANES)
    ahead1 = shifted(s1, "ctx", -1)
    out = rows_block(s0, ahead0, taps, ahead_mask, None, 0, 0, 1024)
    got = exchanged(summed(tied(got, out), 128), None)
    out = rows_block(s0, ahead0, taps, ahead_mask, out, 1024, 1024, w0 - 1024)
    out = rows_block(s1, ahead1, taps, ahead_mask, out, w0, 0, w1)
    filter_grad = last_sum(tied(got, out))[None]
    return out[None], filter_grad


def solution(mesh):
    return jax.shard_map(
        on_device,
        mesh=mesh,
        in_specs=(
            P("section", "ctx", None),
            P("section", "ctx", None),
            P("section", "ctx", None),
            P("section", None, None),
            P("section", None),
        ),
        out_specs=(P("section", "ctx", None), P("section", None, None)),
        check_vma=False,
    )
```

time: 440 us -> 85.2 us (0.19)
  waiting for transfers between devices: 205 us -> 8.73 us
  other arithmetic: 146 us -> 0 us
  local copies, waits for them, and re-layouts: 56.6 us -> 0.66 us
  starting transfers between devices: 15.5 us -> 47 us
  Pallas kernels: 0 us -> 27.5 us
  between operations: 14.2 us -> 0.83 us
    psum x1 -> x0, waiting for transfers between devices: 184 us -> none  [on_device(): filter_grad = lax.psum(local_taps, 'ctx')]
    reduce_sum x144 -> x0, other arithmetic: 65.1 us -> none  [one_turn(): jnp.sum(product, axis=0).reshape(group_count, members).sum(axis=1)]
    add x9 -> x0, other arithmetic: 46.7 us -> none  [the longest x8 46.7 us: one_turn(): grad_rows = grad_rows + term * tap_col[None, :]]
    pallas_call x0 -> x10, Pallas kernels: none -> 27.5 us  [the longest x3 13.5 us: rows_block(): pl.pallas_call(functools.partial(rows_kernel, start, offset, width), in_s...]
    convert_element_type x19 -> x0, other arithmetic: 26.5 us -> none  [the longest x8 13.3 us: one_turn(): lax.dynamic_slice_in_dim(extended, first, tok_rows + lag_block, 0)]
    ppermute x3 -> x6, waiting for transfers between devices: 20.8 us -> 1.12 us  [shifted(): lax.ppermute(value, axis, [(i, (i + steps) % count) for i in range(count)])]
    dynamic_slice x8 -> x0, local copies, waits for them, and re-layouts: 19.3 us -> none  [one_turn(): tap_col = lax.dynamic_slice_in_dim(taps_channel, offset, 1, 1)[:, 0]]
    all_to_all x0 -> x2, starting transfers between devices: none -> 18.7 us  [exchanged(): return lax.all_to_all(value, 'ctx', 0, 0, axis_index_groups=groups)]
  transfers between devices with their start and end apart: 4 -> 8, of which waited for: 3 -> 3; matrix products, arithmetic and copies ran while one was open for 3% -> 0% of each run, Pallas kernels for 0% -> 29%
where the time goes in v1:
time: 85.2 us; the launch traced here: 84.7 us
  starting transfers between devices  47 us (55%)
  Pallas kernels  27.5 us (32%)
  waiting for transfers between devices  8.73 us (10%)
    ppermute x6, starting transfers between devices, shifted(): lax.ppermute(value, axis, [(i, (i + steps) % count) for i in range(count)])  28.2 us
    all_to_all x2, starting transfers between devices, exchanged(): return lax.all_to_all(value, 'ctx', 0, 0, axis_index_groups=groups)  18.7 us
    pallas_call x3, Pallas kernels, rows_block(): pl.pallas_call(functools.partial(rows_kernel, start, offset, width), in_s...  13.5 us
    pallas_call x2, Pallas kernels, taps_block(): pl.pallas_call(functools.partial(taps_kernel, start), in_specs=[VMEM] * l...  7.79 us
    all_to_all x2, waiting for transfers between devices, exchanged(): return lax.all_to_all(value, 'ctx', 0, 0, axis_index_groups=groups)  7.61 us
    pallas_call x2, Pallas kernels, cut(): pl.pallas_call(cut_kernel, in_specs=[pl.BlockSpec(memory_space=pltpu.HBM)...  4.54 us
  transfers between devices with their start and end apart: 8, of which 3 were waited for; matrix products, arithmetic and copies ran while one was open for 0% of the time, Pallas kernels for 29%

profile of v1, /device:TPU:1, one launch (start us, length us, event | category | flops | bytes accessed | tf_op | source)
XLA Modules:
  0.0 84.7 jit_solution(17296573802373828377)
XLA Ops:
  0.6 0.0 copy-start.1
  0.7 2.3 %cut.2 = (bf16[128,2048]{1,0:T(8,128)(2,1)}, bf16[128,2048]{1,0:T(8,128)(2,1)}) custom-call(bf16[128,4096]{1,0:T(8,128)(2,1)} %bitcast.16), custom_call_target="tpu_custom_call" | custom-call | tf_op jit(solution)/shard_map/cut/pallas_call | solution.py:156
  3.0 5.2 %collective-permute-start.2 = (bf16[128,2048]{1,0:T(8,128)(2,1)}, bf16[128,2048]{1,0:T(8,128)(2,1)S(1)}, u32[]{:S(2)}, u32[]{:S(2)}) collective-permute-start(bf16[128,2048]{1,0:T(8,128)(2,1)} %get-tuple-element.17), channel_id=1, source_target_pairs={{0,384},{128,0},{256,128},{384,256},{1,385},{129,1},{257,129},{385... | collective-permute-start | bytes 1572872 | tf_op jit(solution)/shard_map/ppermute | solution.py:232
  8.2 2.2 %cut.3 = (bf16[128,2048]{1,0:T(8,128)(2,1)}, bf16[128,2048]{1,0:T(8,128)(2,1)}) custom-call(bf16[128,4096]{1,0:T(8,128)(2,1)} %bitcast.10), custom_call_target="tpu_custom_call" | custom-call | tf_op jit(solution)/shard_map/cut/pallas_call | solution.py:156
  10.4 4.0 %collective-permute-start.3 = (bf16[128,2048]{1,0:T(8,128)(2,1)}, bf16[128,2048]{1,0:T(8,128)(2,1)S(1)}, u32[]{:S(2)}, u32[]{:S(2)}) collective-permute-start(bf16[128,2048]{1,0:T(8,128)(2,1)} %get-tuple-element.22), channel_id=1, source_target_pairs={{0,1},{1,2},{2,3},{3,4},{4,5},{5,6},{6,7},{7,8},{8,9},{9,10},{10,1... | collective-permute-start | bytes 1572872 | tf_op jit(solution)/shard_map/ppermute | solution.py:232
  14.5 1.9 %collective-permute-start.1 = (bf16[128,2048]{1,0:T(8,128)(2,1)}, bf16[128,2048]{1,0:T(8,128)(2,1)}, u32[]{:S(2)}, u32[]{:S(2)}) collective-permute-start(bf16[128,2048]{1,0:T(8,128)(2,1)} %get-tuple-element.19), channel_id=1, source_target_pairs={{0,1},{1,2},{2,3},{3,4},{4,5},{5,6},{6,7},{7,8},{8,9},{9,10},{10,1... | collective-permute-start | bytes 1572872 | tf_op jit(solution)/shard_map/ppermute | solution.py:232
  16.4 2.5 %collective-permute-start = (bf16[128,2048]{1,0:T(8,128)(2,1)}, bf16[128,2048]{1,0:T(8,128)(2,1)}, u32[]{:S(2)}, u32[]{:S(2)}) collective-permute-start(bf16[128,2048]{1,0:T(8,128)(2,1)} %get-tuple-element.16), channel_id=1, source_target_pairs={{0,384},{128,0},{256,128},{384,256},{1,385},{129,1},{257,129},{385... | collective-permute-start | bytes 1572872 | tf_op jit(solution)/shard_map/ppermute | solution.py:232
  18.9 0.0 copy-start.3
  18.9 0.0 collective-permute-done.2.arr_ref
  18.9 0.6 copy-done.3
  19.5 0.2 masks.1
  19.8 1.1 %collective-permute-done.3.beh_ref = bf16[128,2048]{1,0:T(8,128)(2,1)S(1)} collective-permute-done((bf16[128,2048]{1,0:T(8,128)(2,1)}, bf16[128,2048]{1,0:T(8,128)(2,1)S(1)}, u32[]{:S(2)}, u32[]{:S(2)}) %collective-permute-start.3) | collective-permute-done | bytes 524320 | tf_op jit(solution)/shard_map/ppermute | solution.py:232
  20.9 0.0 copy-done.1
  20.9 3.3 %taps_block_0.1 = (bf16[128,2048]{1,0:T(8,128)(2,1)}, f32[128,128]{1,0:T(8,128)S(1)}) custom-call(bf16[128,2048]{1,0:T(8,128)(2,1)S(1)} %collective-permute-done.2.arr_ref, bf16[128,4096]{1,0:T(8,128)(2,1)S(1)} %bitcast.13, bf16[128,2048]{1,0:T(8,128)(2,1)S(1)} %collective-permute-done.3.beh_ref, bf16[128,4096]{1,0:T(8,128)(2,1)S(1)} %bitcast.11, ...), custom_call_target="tpu_custom_call" | custom-call | flops 72057594037927936 | bytes 4194304 | tf_op jit(solution)/shard_map/taps_block_0/pallas_call | solution.py:67
  24.2 12.5 %collective-permute-start.5 = (bf16[128,2048]{1,0:T(8,128)(2,1)}, bf16[128,2048]{1,0:T(8,128)(2,1)}, u32[]{:S(2)}, u32[]{:S(2)}) collective-permute-start(bf16[128,2048]{1,0:T(8,128)(2,1)} %get-tuple-element.26.s_ref), channel_id=1, source_target_pairs={{0,127},{1,0},{2,1},{3,2},{4,3},{5,4},{6,5},{7,6},{8,7},{9,8},{10,... | collective-permute-start | bytes 1572872 | tf_op jit(solution)/shard_map/ppermute | solution.py:232
  36.6 0.0 collective-permute-done.1.beh_ref
  36.6 0.0 collective-permute-done.arr_ref
  36.6 0.0 copy-start
  36.7 4.5 %taps_block_2048.1 = (bf16[128,2048]{1,0:T(8,128)(2,1)}, bf16[32,8,128]{2,1,0:T(8,128)(2,1)}) custom-call(bf16[128,2048]{1,0:T(8,128)(2,1)} %collective-permute-done.arr_ref, bf16[128,4096]{1,0:T(8,128)(2,1)S(1)} %bitcast.14, bf16[128,2048]{1,0:T(8,128)(2,1)} %collective-permute-done.1.beh_ref, bf16[128,4096]{1,0:T(8,128)(2,1)S(1)} %bitcast.12, ...), custom_call_target="tpu_custom_call" | custom-call | flops 72057594037927936 | bytes 4194304 | tf_op jit(solution)/shard_map/taps_block_2048/pallas_call | solution.py:67
  41.2 4.5 %all-to-all-start = ((bf16[32,8,128]{2,1,0:T(8,128)(2,1)}), bf16[32,8,128]{2,1,0:T(8,128)(2,1)S(1)}, u32[]{:S(2)}, u32[]{:S(2)}) async-start(bf16[32,8,128]{2,1,0:T(8,128)(2,1)} %get-tuple-element.27), calls=%async_computation | async-start | bytes 131072 | tf_op jit(solution)/shard_map/all_to_all | solution.py:236
  45.7 2.1 %collective-permute-start.4 = (bf16[128,2048]{1,0:T(8,128)(2,1)}, bf16[128,2048]{1,0:T(8,128)(2,1)}, u32[]{:S(2)}, u32[]{:S(2)}) collective-permute-start(bf16[128,2048]{1,0:T(8,128)(2,1)} %get-tuple-element.24.s_ref), channel_id=1, source_target_pairs={{0,127},{1,0},{2,1},{3,2},{4,3},{5,4},{6,5},{7,6},{8,7},{9,8},{10,... | collective-permute-start | bytes 1572872 | tf_op jit(solution)/shard_map/ppermute | solution.py:232
  47.8 0.0 collective-permute-done.5.ahead_ref
  47.8 0.0 copy-done
  47.9 3.9 %rows_block_0.1.rest_0_ = bf16[128,4096]{1,0:T(8,128)(2,1)} custom-call(bf16[128,2048]{1,0:T(8,128)(2,1)} %get-tuple-element.26.s_ref, bf16[128,2048]{1,0:T(8,128)(2,1)} %collective-permute-done.5.ahead_ref, f32[256,128]{1,0:T(8,128)S(1)} %bitcast.7, bf16[128,256]{1,0:T(8,128)(2,1)S(1)} %get-tuple-element.25.mask_ref), custom_call_target="tpu_custom_call" | custom-call | flops 268435456 | bytes 1048576 | tf_op jit(solution)/shard_map/rows_block_0/pallas_call | solution.py:108
  51.8 2.0 %all-to-all-done.parts_ref = bf16[32,8,128]{2,1,0:T(8,128)(2,1)S(1)} async-done(((bf16[32,8,128]{2,1,0:T(8,128)(2,1)}), bf16[32,8,128]{2,1,0:T(8,128)(2,1)S(1)}, u32[]{:S(2)}, u32[]{:S(2)}) %all-to-all-start) | async-done | bytes 65568 | tf_op jit(solution)/shard_map/all_to_all | solution.py:236
  53.8 0.8 sum_of_32.1
  54.5 14.3 %all-to-all-start.1 = ((bf16[128,8,128]{2,1,0:T(8,128)(2,1)}), bf16[128,8,128]{2,1,0:T(8,128)(2,1)S(1)}, u32[]{:S(2)}, u32[]{:S(2)}) async-start(bf16[128,8,128]{2,1,0:T(8,128)(2,1)} %sum_of_32.1), calls=%async_computation.1 | async-start | bytes 524288 | tf_op jit(solution)/shard_map/all_to_all | solution.py:236
  68.8 3.9 %rows_block_1024.1.rest_0_ = bf16[128,4096]{1,0:T(8,128)(2,1)} custom-call(bf16[128,2048]{1,0:T(8,128)(2,1)} %get-tuple-element.26.s_ref, bf16[128,2048]{1,0:T(8,128)(2,1)} %collective-permute-done.5.ahead_ref, f32[256,128]{1,0:T(8,128)S(1)} %bitcast.8, bf16[128,256]{1,0:T(8,128)(2,1)S(1)} %get-tuple-element.25.mask_ref, ...), custom_call_target="tpu_custom_call", output_to_operand_aliasing={{}: (4, {})} | custom-call | flops 268435456 | bytes 1048576 | tf_op jit(solution)/shard_map/rows_block_1024/pallas_call | solution.py:108
  72.7 0.0 collective-permute-done.4.ahead_ref
  72.7 5.7 %rows_block_2048.1 = bf16[128,4096]{1,0:T(8,128)(2,1)} custom-call(bf16[128,2048]{1,0:T(8,128)(2,1)} %get-tuple-element.24.s_ref, bf16[128,2048]{1,0:T(8,128)(2,1)} %collective-permute-done.4.ahead_ref, f32[256,128]{1,0:T(8,128)S(1)} %bitcast.9, bf16[128,256]{1,0:T(8,128)(2,1)S(1)} %get-tuple-element.25.mask_ref, ...), custom_call_target="tpu_custom_call", output_to_operand_aliasing={{}: (4, {})} | custom-call | flops 536870912 | bytes 2097152 | tf_op jit(solution)/shard_map/rows_block_2048/pallas_call | solution.py:108
  78.4 5.6 %all-to-all-done.1.parts_ref = bf16[128,8,128]{2,1,0:T(8,128)(2,1)S(1)} async-done(((bf16[128,8,128]{2,1,0:T(8,128)(2,1)}), bf16[128,8,128]{2,1,0:T(8,128)(2,1)S(1)}, u32[]{:S(2)}, u32[]{:S(2)}) %all-to-all-start.1) | async-done | bytes 262176 | tf_op jit(solution)/shard_map/all_to_all | solution.py:236
  84.0 0.7 last_sum.1
  (2 shorter events, 0.0 us)
Async XLA Ops:
  0.6 20.3 %copy-start.1 = (bf16[1,128,4096]{2,1,0:T(8,128)(2,1)S(1)}, bf16[1,128,4096]{2,1,0:T(8,128)(2,1)}, u32[]{:S(2)}) copy-start(bf16[1,128,4096]{2,1,0:T(8,128)(2,1)} %param.6) | copy-start | bytes 3145732
  0.6 20.3 %copy-start.2 = (bf16[1,128,4096]{2,1,0:T(8,128)(2,1)S(1)}, bf16[1,128,4096]{2,1,0:T(8,128)(2,1)}, u32[]{:S(2)}) copy-start(bf16[1,128,4096]{2,1,0:T(8,128)(2,1)} %param.5) | copy-start | bytes 3145732
  3.0 15.9 %collective-permute-start.2 = (bf16[128,2048]{1,0:T(8,128)(2,1)}, bf16[128,2048]{1,0:T(8,128)(2,1)S(1)}, u32[]{:S(2)}, u32[]{:S(2)}) collective-permute-start(bf16[128,2048]{1,0:T(8,128)(2,1)} %get-tuple-element.17), channel_id=1, source_target_pairs={{0,384},{128,0},{256,128},{384,256},{1,385},{129,1},{257,129},{385... | collective-permute-start | bytes 1572872 | tf_op jit(solution)/shard_map/ppermute | solution.py:232
  10.4 10.5 %collective-permute-start.3 = (bf16[128,2048]{1,0:T(8,128)(2,1)}, bf16[128,2048]{1,0:T(8,128)(2,1)S(1)}, u32[]{:S(2)}, u32[]{:S(2)}) collective-permute-start(bf16[128,2048]{1,0:T(8,128)(2,1)} %get-tuple-element.22), channel_id=1, source_target_pairs={{0,1},{1,2},{2,3},{3,4},{4,5},{5,6},{6,7},{7,8},{8,9},{9,10},{10,1... | collective-permute-start | bytes 1572872 | tf_op jit(solution)/shard_map/ppermute | solution.py:232
  14.5 22.1 %collective-permute-start.1 = (bf16[128,2048]{1,0:T(8,128)(2,1)}, bf16[128,2048]{1,0:T(8,128)(2,1)}, u32[]{:S(2)}, u32[]{:S(2)}) collective-permute-start(bf16[128,2048]{1,0:T(8,128)(2,1)} %get-tuple-element.19), channel_id=1, source_target_pairs={{0,1},{1,2},{2,3},{3,4},{4,5},{5,6},{6,7},{7,8},{8,9},{9,10},{10,1... | collective-permute-start | bytes 1572872 | tf_op jit(solution)/shard_map/ppermute | solution.py:232
  16.4 20.2 %collective-permute-start = (bf16[128,2048]{1,0:T(8,128)(2,1)}, bf16[128,2048]{1,0:T(8,128)(2,1)}, u32[]{:S(2)}, u32[]{:S(2)}) collective-permute-start(bf16[128,2048]{1,0:T(8,128)(2,1)} %get-tuple-element.16), channel_id=1, source_target_pairs={{0,384},{128,0},{256,128},{384,256},{1,385},{129,1},{257,129},{385... | collective-permute-start | bytes 1572872 | tf_op jit(solution)/shard_map/ppermute | solution.py:232
  18.9 0.7 copy-start.3
  24.2 23.7 %collective-permute-start.5 = (bf16[128,2048]{1,0:T(8,128)(2,1)}, bf16[128,2048]{1,0:T(8,128)(2,1)}, u32[]{:S(2)}, u32[]{:S(2)}) collective-permute-start(bf16[128,2048]{1,0:T(8,128)(2,1)} %get-tuple-element.26.s_ref), channel_id=1, source_target_pairs={{0,127},{1,0},{2,1},{3,2},{4,3},{5,4},{6,5},{7,6},{8,7},{9,8},{10,... | collective-permute-start | bytes 1572872 | tf_op jit(solution)/shard_map/ppermute | solution.py:232
  36.6 11.2 %copy-start = (f32[1,256,128]{2,1,0:T(8,128)S(1)}, f32[1,256,128]{2,1,0:T(8,128)}, u32[]{:S(2)}) copy-start(f32[1,256,128]{2,1,0:T(8,128)} %param.8) | copy-start | bytes 393220
  41.2 12.6 %all-to-all-start = ((bf16[32,8,128]{2,1,0:T(8,128)(2,1)}), bf16[32,8,128]{2,1,0:T(8,128)(2,1)S(1)}, u32[]{:S(2)}, u32[]{:S(2)}) async-start(bf16[32,8,128]{2,1,0:T(8,128)(2,1)} %get-tuple-element.27), calls=%async_computation | async-start | bytes 131072 | tf_op jit(solution)/shard_map/all_to_all | solution.py:236
  45.7 27.0 %collective-permute-start.4 = (bf16[128,2048]{1,0:T(8,128)(2,1)}, bf16[128,2048]{1,0:T(8,128)(2,1)}, u32[]{:S(2)}, u32[]{:S(2)}) collective-permute-start(bf16[128,2048]{1,0:T(8,128)(2,1)} %get-tuple-element.24.s_ref), channel_id=1, source_target_pairs={{0,127},{1,0},{2,1},{3,2},{4,3},{5,4},{6,5},{7,6},{8,7},{9,8},{10,... | collective-permute-start | bytes 1572872 | tf_op jit(solution)/shard_map/ppermute | solution.py:232
  54.5 29.5 %all-to-all-start.1 = ((bf16[128,8,128]{2,1,0:T(8,128)(2,1)}), bf16[128,8,128]{2,1,0:T(8,128)(2,1)S(1)}, u32[]{:S(2)}, u32[]{:S(2)}) async-start(bf16[128,8,128]{2,1,0:T(8,128)(2,1)} %sum_of_32.1), calls=%async_computation.1 | async-start | bytes 524288 | tf_op jit(solution)/shard_map/all_to_all | solution.py:236

commit v2 on v1

--- a/solution.py
+++ b/solution.py
@@ -9,7 +9,7 @@
 BF, F32 = jnp.bfloat16, jnp.float32
 TOK, CH, GRP, TAPS, FILT = 128, 4096, 16, 128, 256
 VMEM = pl.BlockSpec(memory_space=pltpu.VMEM)
-ROOM = 16 * 1024 * 1024
+ROOM = 12 * 1024 * 1024
 
 
 def lag_sums(products, flip):
@@ -23,22 +23,20 @@
     return jnp.concatenate(rows, axis=0)
 
 
-def taps_kernel(start, arr_ref, gate_ref, beh_ref, own_ref, mask_ref, *rest):
-    acc_ref = rest[-1]
-    width = arr_ref.shape[1]
+def taps_kernel(arr_ref, gate_ref, beh_ref, own_ref, mask_ref, s0_ref, s1_ref, g_ref, acc_ref):
     mask = mask_ref[...]
     row = lax.broadcasted_iota(jnp.int32, (TOK, TOK), 0)
     lane = lax.broadcasted_iota(jnp.int32, (TOK, TOK), 1)
     tri = lane <= row
     flip = ((row + lane) % TAPS == 0).astype(F32).astype(BF)
     chosen = (lane[:8] // GRP == row[:8]).astype(F32).astype(BF)
-    s_ref, g_ref = rest[-3:-1]
-    for h in range(width // 128):
+    for h in range(CH // 128):
         here = slice(128 * h, 128 * h + 128)
-        there = slice(start + 128 * h, start + 128 * h + 128)
-        s = (arr_ref[:, here].astype(F32) * gate_ref[:, there].astype(F32)).astype(BF)
-        s_ref[:, here] = s
-        past = jnp.concatenate([beh_ref[:, here], own_ref[:, there]], axis=0)
+        s = (arr_ref[:, here].astype(F32) * gate_ref[:, here].astype(F32)).astype(BF)
+        s_ref = s0_ref if h < CH // 256 else s1_ref
+        at = 128 * h % (CH // 2)
+        s_ref[:, at : at + 128] = s
+        past = jnp.concatenate([beh_ref[:, here], own_ref[:, here]], axis=0)
         for g in range(8):
             one = s * chosen[g : g + 1, :]
             prod = lax.dot_general(one, past, (((1,), (1,)), ((), ())), preferred_element_type=F32)
@@ -48,32 +46,23 @@
                 part = part + pltpu.roll(both[8 * a : 8 * a + 8], 128 - 8 * a, 1)
             acc_ref[64 * h + 8 * g : 64 * h + 8 * g + 8, :] = part
     sums = lag_sums(acc_ref[...], flip)
-    if len(g_ref.shape) == 2:
-        g_ref[...] = sums
-    else:
-        whole = jnp.concatenate([r[...] for r in rest[:-3]] + [sums], axis=0)
-        n, per = g_ref.shape[:2]
-        for i in range(n):
-            g_ref[i] = whole[per * i : per * i + per].astype(BF)
-
-
-def taps_block(arr, gate, behind, own, mask, start, before=(), parts=None):
-    width = arr.shape[1]
-    if parts:
-        sums = jax.ShapeDtypeStruct((parts, FILT // parts, TAPS), BF)
-    else:
-        sums = jax.ShapeDtypeStruct((width // GRP, TAPS), F32)
-    args = (arr, gate, *behind, own, mask, *before)
-    return pl.pallas_call(
-        functools.partial(taps_kernel, start),
-        in_specs=[VMEM] * len(args),
-        out_specs=[VMEM, VMEM],
-        out_shape=[jax.ShapeDtypeStruct((TOK, width), BF), sums],
-        scratch_shapes=[pltpu.VMEM((width // 2, 128), F32)],
-        compiler_params=pltpu.CompilerParams(vmem_limit_bytes=ROOM),
-        cost_estimate=pl.CostEstimate(flops=1 << 56, bytes_accessed=width << 11, transcendentals=0),
-        name=f"taps_block_{start}",
-    )(*args)
+    per = g_ref.shape[1]
+    for i in range(g_ref.shape[0]):
+        g_ref[i] = sums[per * i : per * i + per].astype(BF)
+
+
+def taps_sums(arr, gate, behind, own, mask, parts):
+    half = jax.ShapeDtypeStruct((TOK, CH // 2), BF)
+    return pl.pallas_call(
+        taps_kernel,
+        in_specs=[VMEM] * 5,
+        out_specs=[VMEM] * 3,
+        out_shape=[half, half, jax.ShapeDtypeStruct((parts, FILT // parts, TAPS), BF)],
+        scratch_shapes=[pltpu.VMEM((CH // 2, 128), F32)],
+        compiler_params=pltpu.CompilerParams(vmem_limit_bytes=ROOM),
+        cost_estimate=pl.CostEstimate(flops=CH << 18, bytes_accessed=CH << 11, transcendentals=0),
+        name="taps_sums",
+    )(arr, gate, behind, own, mask)
 
 
 def rows_kernel(start, offset, width, s_ref, ahead_ref, taps_ref, mask_ref, *rest):
@@ -113,7 +102,7 @@
         input_output_aliases={4: 0} if out is not None else {},
         scratch_shapes=[pltpu.VMEM((TOK, width), BF), pltpu.SemaphoreType.DMA(())],
         compiler_params=pltpu.CompilerParams(vmem_limit_bytes=ROOM),
-        cost_estimate=pl.CostEstimate(flops=width << 18, bytes_accessed=width << 10, transcendentals=0),
+        cost_estimate=pl.CostEstimate(flops=1 << 35, bytes_accessed=width << 10, transcendentals=0),
         name=f"rows_block_{start}",
     )(*args)
 
@@ -134,34 +123,34 @@
         out_specs=VMEM,
         out_shape=jax.ShapeDtypeStruct((copies,) + parts.shape[1:], BF),
         compiler_params=pltpu.CompilerParams(vmem_limit_bytes=ROOM),
-        cost_estimate=pl.CostEstimate(flops=1 << 56, bytes_accessed=parts.size * 2, transcendentals=0),
+        cost_estimate=pl.CostEstimate(flops=1 << 35, bytes_accessed=parts.size * 2, transcendentals=0),
         name=f"sum_of_{parts.shape[0]}",
     )(parts)
 
 
-def cut_kernel(whole_ref, *rest):
-    n = len(rest) // 2
-    copies, at = [], 0
-    for i in range(n):
-        width = rest[i].shape[1]
-        copies.append(pltpu.make_async_copy(whole_ref.at[:, pl.ds(at, width)], rest[i], rest[n + i]))
-        at += width
+def held_kernel(gate_ref, own_ref, gate_out, own_out, sems):
+    copies = [
+        pltpu.make_async_copy(gate_ref, gate_out, sems.at[0]),
+        pltpu.make_async_copy(own_ref, own_out, sems.at[1]),
+    ]
     for copy in copies:
         copy.start()
     for copy in copies:
         copy.wait()
 
 
-def cut(whole, widths):
-    return pl.pallas_call(
-        cut_kernel,
-        in_specs=[pl.BlockSpec(memory_space=pltpu.HBM)],
-        out_specs=[VMEM] * len(widths),
-        out_shape=[jax.ShapeDtypeStruct((TOK, w), BF) for w in widths],
-        scratch_shapes=[pltpu.SemaphoreType.DMA(()) for _ in widths],
-        compiler_params=pltpu.CompilerParams(vmem_limit_bytes=56 * 1024 * 1024),
-        name="cut",
-    )(whole)
+def held(gate, own):
+    block = jax.ShapeDtypeStruct((TOK, CH), BF)
+    return pl.pallas_call(
+        held_kernel,
+        in_specs=[pl.BlockSpec(memory_space=pltpu.HBM)] * 2,
+        out_specs=[VMEM] * 2,
+        out_shape=[block, block],
+        scratch_shapes=[pltpu.SemaphoreType.DMA((2,))],
+        compiler_params=pltpu.CompilerParams(vmem_limit_bytes=4 * 1024 * 1024),
+        cost_estimate=pl.CostEstimate(flops=1 << 30, bytes_accessed=4 << 20, transcendentals=0),
+        name="held",
+    )(gate, own)
 
 
 def mask_kernel(base_ref, len_ref, ahead_ref, behind_ref):
@@ -217,9 +206,6 @@
     )(parts)
 
 
-WIDTHS = (2048, 2048)
-
-
 def place(z, y, c):
     return (z * 8 + y) * 2 + c
 
@@ -227,9 +213,11 @@
 PLANES = [[place(z + i, y, c) for i in range(2) for y in range(8) for c in range(2)] for z in range(0, 8, 2)]
 
 
-def shifted(value, axis, steps):
+def shifted(value, axis, steps, around=False):
     count = lax.axis_size(axis)
-    return lax.ppermute(value, axis, [(i, (i + steps) % count) for i in range(count)])
+    pairs = [(i, i + steps) for i in range(count)]
+    pairs = [(i, j % count) for i, j in pairs if around or 0 <= j < count]
+    return lax.ppermute(value, axis, pairs)
 
 
 def exchanged(value, groups):
@@ -243,21 +231,18 @@
 def on_device(gate_values, conv_input, sent_grads, filter_taps, doc_lengths):
     gate, conv, sent, taps = gate_values[0], conv_input[0], sent_grads[0], filter_taps[0]
     base = lax.axis_index("ctx") * TOK
-    w0, w1 = WIDTHS
-    piece0, piece1 = cut(sent, WIDTHS)
-    arr0 = shifted(piece0, "section", -1)
-    arr1 = shifted(piece1, "section", -1)
-    behind = [shifted(piece, "ctx", 1) for piece in cut(tied(conv, piece0), (CH // 2, CH // 2))]
-    ahead_mask, behind_mask = masks(tied(doc_lengths, arr0), base)
-    s0, g0 = taps_block(arr0, gate, behind[:1], conv, behind_mask, 0)
+    half = CH // 2
+    arrived = shifted(sent, "section", -1, around=True)
+    behind = shifted(conv, "ctx", 1)
+    gate, own = held(gate, conv)
+    ahead_mask, behind_mask = masks(tied(doc_lengths, arrived), base)
+    s0, s1, local = taps_sums(arrived, gate, behind, own, behind_mask, 32)
+    got = exchanged(local, PLANES)
     ahead0 = shifted(s0, "ctx", -1)
-    s1, local = taps_block(arr1, gate, behind[1:], conv, behind_mask, w0, (g0,), 32)
-    got = exchanged(local, PLANES)
     ahead1 = shifted(s1, "ctx", -1)
-    out = rows_block(s0, ahead0, taps, ahead_mask, None, 0, 0, 1024)
-    got = exchanged(summed(tied(got, out), 128), None)
-    out = rows_block(s0, ahead0, taps, ahead_mask, out, 1024, 1024, w0 - 1024)
-    out = rows_block(s1, ahead1, taps, ahead_mask, out, w0, 0, w1)
+    got = exchanged(summed(got, 128), None)
+    out = rows_block(s0, ahead0, taps, ahead_mask, None, 0, 0, half)
+    out = rows_block(s1, ahead1, taps, ahead_mask, out, half, 0, half)
     filter_grad = last_sum(tied(got, out))[None]
     return out[None], filter_grad
 

time: 85.2 us -> 82.4 us (0.967)
  waiting for transfers between devices: 8.73 us -> 22.9 us
  Pallas kernels: 27.5 us -> 16.6 us
  starting transfers between devices: 47 us -> 39.4 us
  local copies, waits for them, and re-layouts: 0.66 us -> 2.45 us
    ppermute x6 -> x4, starting transfers between devices: 28.2 us -> 13.3 us  [shifted(): return lax.ppermute(value, axis, pairs)]
    ppermute x6 -> x4, waiting for transfers between devices: 1.12 us -> 12.8 us  [shifted(): return lax.ppermute(value, axis, pairs)]
    all_to_all x2, starting transfers between devices: 18.7 us -> 26 us  [exchanged(): return lax.all_to_all(value, 'ctx', 0, 0, axis_index_groups=groups)]
    pallas_call x4 -> x2, Pallas kernels: 12.3 us -> 5.78 us  [the longest x1 5.62 us: taps_sums(): pl.pallas_call(taps_kernel, in_specs=[VMEM] * 5, out_specs=[VMEM] * 3, ou...]
    pallas_call x3 -> x2, Pallas kernels: 13.5 us -> 9.09 us  [rows_block(): pl.pallas_call(functools.partial(rows_kernel, start, offset, width), in_s...]
    all_to_all x2, waiting for transfers between devices: 7.61 us -> 10.1 us  [exchanged(): return lax.all_to_all(value, 'ctx', 0, 0, axis_index_groups=groups)]
    unnamed x8, local copies, waits for them, and re-layouts: 0.66 us -> 2.45 us
  transfers between devices with their start and end apart: 8 -> 6, of which waited for: 3 -> 3; matrix products, arithmetic and copies ran while one was open for 0% -> 0% of each run, Pallas kernels for 29% -> 13%
where the time goes in v2:
time: 82.4 us; the launch traced here: 82 us
  starting transfers between devices  39.4 us (48%)
  waiting for transfers between devices  22.9 us (28%)
  Pallas kernels  16.6 us (20%)
  local copies, waits for them, and re-layouts  2.45 us (3%)
    all_to_all x2, starting transfers between devices, exchanged(): return lax.all_to_all(value, 'ctx', 0, 0, axis_index_groups=groups)  26 us
    ppermute x4, starting transfers between devices, shifted(): return lax.ppermute(value, axis, pairs)  13.3 us
    ppermute x4, waiting for transfers between devices, shifted(): return lax.ppermute(value, axis, pairs)  12.8 us
    all_to_all x2, waiting for transfers between devices, exchanged(): return lax.all_to_all(value, 'ctx', 0, 0, axis_index_groups=groups)  10.1 us
    pallas_call x2, Pallas kernels, rows_block(): pl.pallas_call(functools.partial(rows_kernel, start, offset, width), in_s...  9.09 us
    pallas_call x1, Pallas kernels, taps_sums(): pl.pallas_call(taps_kernel, in_specs=[VMEM] * 5, out_specs=[VMEM] * 3, ou...  5.62 us
    unnamed x8, local copies, waits for them, and re-layouts  2.45 us
  transfers between devices with their start and end apart: 6, of which 3 were waited for; matrix products, arithmetic and copies ran while one was open for 0% of the time, Pallas kernels for 13%

profile of v2, /device:TPU:1, one launch (start us, length us, event | category | flops | bytes accessed | tf_op | source)
XLA Modules:
  0.0 82.0 jit_solution(4461221310472550728)
XLA Ops:
  0.6 5.2 %collective-permute-start = (bf16[128,4096]{1,0:T(8,128)(2,1)}, bf16[128,4096]{1,0:T(8,128)(2,1)S(1)}, u32[]{:S(2)}, u32[]{:S(2)}) collective-permute-start(bf16[128,4096]{1,0:T(8,128)(2,1)} %bitcast.13), channel_id=1, source_target_pairs={{0,384},{128,0},{256,128},{384,256},{1,385},{129,1},{257,129},{385... | collective-permute-start | bytes 3145736 | tf_op jit(solution)/shard_map/ppermute | solution.py:220
  5.9 4.0 %collective-permute-start.1 = (bf16[128,4096]{1,0:T(8,128)(2,1)}, bf16[128,4096]{1,0:T(8,128)(2,1)S(1)}, u32[]{:S(2)}, u32[]{:S(2)}) collective-permute-start(bf16[128,4096]{1,0:T(8,128)(2,1)} %bitcast.8), channel_id=1, source_target_pairs={{0,1},{1,2},{2,3},{3,4},{4,5},{5,6},{6,7},{7,8},{8,9},{9,10},{10,1... | collective-permute-start | bytes 3145736 | tf_op jit(solution)/shard_map/ppermute | solution.py:220
  9.9 0.0 copy-start
  9.9 1.2 %copy-done = bf16[1,128,4096]{2,1,0:T(8,128)(2,1)S(1)} copy-done((bf16[1,128,4096]{2,1,0:T(8,128)(2,1)S(1)}, bf16[1,128,4096]{2,1,0:T(8,128)(2,1)}, u32[]{:S(2)}) %copy-start) | copy-done | bytes 1048600
  11.1 0.0 copy-start.1
  11.1 1.2 %copy-done.1 = bf16[1,128,4096]{2,1,0:T(8,128)(2,1)S(1)} copy-done((bf16[1,128,4096]{2,1,0:T(8,128)(2,1)S(1)}, bf16[1,128,4096]{2,1,0:T(8,128)(2,1)}, u32[]{:S(2)}) %copy-start.1) | copy-done | bytes 1048600
  12.4 0.2 held.1
  12.5 0.0 copy-start.3
  12.5 12.8 %collective-permute-done.arr_ref = bf16[128,4096]{1,0:T(8,128)(2,1)S(1)} collective-permute-done((bf16[128,4096]{1,0:T(8,128)(2,1)}, bf16[128,4096]{1,0:T(8,128)(2,1)S(1)}, u32[]{:S(2)}, u32[]{:S(2)}) %collective-permute-start) | collective-permute-done | bytes 1048608 | tf_op jit(solution)/shard_map/ppermute | solution.py:220
  25.3 0.0 copy-done.3
  25.3 0.2 masks.1
  25.6 0.0 collective-permute-done.1.beh_ref
  25.6 5.6 %taps_sums.1 = (bf16[128,2048]{1,0:T(8,128)(2,1)S(1)}, bf16[128,2048]{1,0:T(8,128)(2,1)S(1)}, bf16[32,8,128]{2,1,0:T(8,128)(2,1)}) custom-call(bf16[128,4096]{1,0:T(8,128)(2,1)S(1)} %collective-permute-done.arr_ref, bf16[128,4096]{1,0:T(8,128)(2,1)S(1)} %get-tuple-element.11.gate_ref, bf16[128,4096]{1,0:T(8,128)(2,1)S(1)} %collective-permute-done.1.beh_ref, ...), custom_call_target="tpu_custom_call" | custom-call | flops 1073741824 | bytes 8388608 | tf_op jit(solution)/shard_map/taps_sums/pallas_call | solution.py:56
  31.2 13.3 %all-to-all-start = ((bf16[32,8,128]{2,1,0:T(8,128)(2,1)}), bf16[32,8,128]{2,1,0:T(8,128)(2,1)S(1)}, u32[]{:S(2)}, u32[]{:S(2)}) async-start(bf16[32,8,128]{2,1,0:T(8,128)(2,1)} %get-tuple-element.18), calls=%async_computation | async-start | bytes 131072 | tf_op jit(solution)/shard_map/all_to_all | solution.py:224
  44.5 2.1 %collective-permute-start.2 = (bf16[128,2048]{1,0:T(8,128)(2,1)S(1)}, bf16[128,2048]{1,0:T(8,128)(2,1)S(1)}, u32[]{:S(2)}, u32[]{:S(2)}) collective-permute-start(bf16[128,2048]{1,0:T(8,128)(2,1)S(1)} %get-tuple-element.15.s_ref), channel_id=1, source_target_pairs={{1,0},{2,1},{3,2},{4,3},{5,4},{6,5},{7,6},{8,7},{9,8},{10,9},{11,1... | collective-permute-start | bytes 1572872 | tf_op jit(solution)/shard_map/ppermute | solution.py:220
  46.6 1.9 %collective-permute-start.3 = (bf16[128,2048]{1,0:T(8,128)(2,1)S(1)}, bf16[128,2048]{1,0:T(8,128)(2,1)S(1)}, u32[]{:S(2)}, u32[]{:S(2)}) collective-permute-start(bf16[128,2048]{1,0:T(8,128)(2,1)S(1)} %get-tuple-element.17.s_ref), channel_id=1, source_target_pairs={{1,0},{2,1},{3,2},{4,3},{5,4},{6,5},{7,6},{8,7},{9,8},{10,9},{11,1... | collective-permute-start | bytes 1572872 | tf_op jit(solution)/shard_map/ppermute | solution.py:220
  48.6 4.0 %all-to-all-done.parts_ref = bf16[32,8,128]{2,1,0:T(8,128)(2,1)S(1)} async-done(((bf16[32,8,128]{2,1,0:T(8,128)(2,1)}), bf16[32,8,128]{2,1,0:T(8,128)(2,1)S(1)}, u32[]{:S(2)}, u32[]{:S(2)}) %all-to-all-start) | async-done | bytes 65568 | tf_op jit(solution)/shard_map/all_to_all | solution.py:224
  52.6 0.8 sum_of_32.1
  53.3 0.0 copy-start.2
  53.3 12.7 %all-to-all-start.1 = ((bf16[128,8,128]{2,1,0:T(8,128)(2,1)}), bf16[128,8,128]{2,1,0:T(8,128)(2,1)S(1)}, u32[]{:S(2)}, u32[]{:S(2)}) async-start(bf16[128,8,128]{2,1,0:T(8,128)(2,1)} %sum_of_32.1), calls=%async_computation.1 | async-start | bytes 524288 | tf_op jit(solution)/shard_map/all_to_all | solution.py:224
  66.1 0.0 collective-permute-done.3.ahead_ref
  66.1 0.0 copy-done.2
  66.1 4.5 %rows_block_0.1.rest_0_ = bf16[128,4096]{1,0:T(8,128)(2,1)} custom-call(bf16[128,2048]{1,0:T(8,128)(2,1)S(1)} %get-tuple-element.17.s_ref, bf16[128,2048]{1,0:T(8,128)(2,1)S(1)} %collective-permute-done.3.ahead_ref, f32[256,128]{1,0:T(8,128)S(1)} %bitcast.10, bf16[128,256]{1,0:T(8,128)(2,1)S(1)} %get-tuple-element.16.mask_ref), custom_call_target="tpu_custom_call" | custom-call | flops 34359738368 | bytes 2097152 | tf_op jit(solution)/shard_map/rows_block_0/pallas_call | solution.py:97
  70.6 0.0 collective-permute-done.2.ahead_ref
  70.6 4.5 %rows_block_2048.1 = bf16[128,4096]{1,0:T(8,128)(2,1)} custom-call(bf16[128,2048]{1,0:T(8,128)(2,1)S(1)} %get-tuple-element.15.s_ref, bf16[128,2048]{1,0:T(8,128)(2,1)S(1)} %collective-permute-done.2.ahead_ref, f32[256,128]{1,0:T(8,128)S(1)} %bitcast.11, bf16[128,256]{1,0:T(8,128)(2,1)S(1)} %get-tuple-element.16.mask_ref, ...), custom_call_target="tpu_custom_call", output_to_operand_aliasing={{}: (4, {})} | custom-call | flops 34359738368 | bytes 2097152 | tf_op jit(solution)/shard_map/rows_block_2048/pallas_call | solution.py:97
  75.2 6.1 %all-to-all-done.1.parts_ref = bf16[128,8,128]{2,1,0:T(8,128)(2,1)S(1)} async-done(((bf16[128,8,128]{2,1,0:T(8,128)(2,1)}), bf16[128,8,128]{2,1,0:T(8,128)(2,1)S(1)}, u32[]{:S(2)}, u32[]{:S(2)}) %all-to-all-start.1) | async-done | bytes 262176 | tf_op jit(solution)/shard_map/all_to_all | solution.py:224
  81.3 0.7 last_sum.1
Async XLA Ops:
  0.6 24.7 %collective-permute-start = (bf16[128,4096]{1,0:T(8,128)(2,1)}, bf16[128,4096]{1,0:T(8,128)(2,1)S(1)}, u32[]{:S(2)}, u32[]{:S(2)}) collective-permute-start(bf16[128,4096]{1,0:T(8,128)(2,1)} %bitcast.13), channel_id=1, source_target_pairs={{0,384},{128,0},{256,128},{384,256},{1,385},{129,1},{257,129},{385... | collective-permute-start | bytes 3145736 | tf_op jit(solution)/shard_map/ppermute | solution.py:220
  5.9 19.7 %collective-permute-start.1 = (bf16[128,4096]{1,0:T(8,128)(2,1)}, bf16[128,4096]{1,0:T(8,128)(2,1)S(1)}, u32[]{:S(2)}, u32[]{:S(2)}) collective-permute-start(bf16[128,4096]{1,0:T(8,128)(2,1)} %bitcast.8), channel_id=1, source_target_pairs={{0,1},{1,2},{2,3},{3,4},{4,5},{5,6},{6,7},{7,8},{8,9},{9,10},{10,1... | collective-permute-start | bytes 3145736 | tf_op jit(solution)/shard_map/ppermute | solution.py:220
  9.9 1.2 %copy-start = (bf16[1,128,4096]{2,1,0:T(8,128)(2,1)S(1)}, bf16[1,128,4096]{2,1,0:T(8,128)(2,1)}, u32[]{:S(2)}) copy-start(bf16[1,128,4096]{2,1,0:T(8,128)(2,1)} %param.5) | copy-start | bytes 3145732
  11.1 1.2 %copy-start.1 = (bf16[1,128,4096]{2,1,0:T(8,128)(2,1)S(1)}, bf16[1,128,4096]{2,1,0:T(8,128)(2,1)}, u32[]{:S(2)}) copy-start(bf16[1,128,4096]{2,1,0:T(8,128)(2,1)} %param.6) | copy-start | bytes 3145732
  12.5 12.8 %copy-start.3 = (s32[1,128]{1,0:T(1,128)S(1)}, s32[1,128]{1,0:T(1,128)}, u32[]{:S(2)}) copy-start(s32[1,128]{1,0:T(1,128)} %len_ref) | copy-start | bytes 1540
  31.2 21.4 %all-to-all-start = ((bf16[32,8,128]{2,1,0:T(8,128)(2,1)}), bf16[32,8,128]{2,1,0:T(8,128)(2,1)S(1)}, u32[]{:S(2)}, u32[]{:S(2)}) async-start(bf16[32,8,128]{2,1,0:T(8,128)(2,1)} %get-tuple-element.18), calls=%async_computation | async-start | bytes 131072 | tf_op jit(solution)/shard_map/all_to_all | solution.py:224
  44.5 26.2 %collective-permute-start.2 = (bf16[128,2048]{1,0:T(8,128)(2,1)S(1)}, bf16[128,2048]{1,0:T(8,128)(2,1)S(1)}, u32[]{:S(2)}, u32[]{:S(2)}) collective-permute-start(bf16[128,2048]{1,0:T(8,128)(2,1)S(1)} %get-tuple-element.15.s_ref), channel_id=1, source_target_pairs={{1,0},{2,1},{3,2},{4,3},{5,4},{6,5},{7,6},{8,7},{9,8},{10,9},{11,1... | collective-permute-start | bytes 1572872 | tf_op jit(solution)/shard_map/ppermute | solution.py:220
  46.6 19.4 %collective-permute-start.3 = (bf16[128,2048]{1,0:T(8,128)(2,1)S(1)}, bf16[128,2048]{1,0:T(8,128)(2,1)S(1)}, u32[]{:S(2)}, u32[]{:S(2)}) collective-permute-start(bf16[128,2048]{1,0:T(8,128)(2,1)S(1)} %get-tuple-element.17.s_ref), channel_id=1, source_target_pairs={{1,0},{2,1},{3,2},{4,3},{5,4},{6,5},{7,6},{8,7},{9,8},{10,9},{11,1... | collective-permute-start | bytes 1572872 | tf_op jit(solution)/shard_map/ppermute | solution.py:220
  53.3 12.8 %copy-start.2 = (f32[1,256,128]{2,1,0:T(8,128)S(1)}, f32[1,256,128]{2,1,0:T(8,128)}, u32[]{:S(2)}) copy-start(f32[1,256,128]{2,1,0:T(8,128)} %param.8) | copy-start | bytes 393220
  53.3 28.0 %all-to-all-start.1 = ((bf16[128,8,128]{2,1,0:T(8,128)(2,1)}), bf16[128,8,128]{2,1,0:T(8,128)(2,1)S(1)}, u32[]{:S(2)}, u32[]{:S(2)}) async-start(bf16[128,8,128]{2,1,0:T(8,128)(2,1)} %sum_of_32.1), calls=%async_computation.1 | async-start | bytes 524288 | tf_op jit(solution)/shard_map/all_to_all | solution.py:224

commit v3 on v2

--- a/solution.py
+++ b/solution.py
@@ -12,15 +12,14 @@
 ROOM = 12 * 1024 * 1024
 
 
-def lag_sums(products, flip):
-    hi = products.astype(BF)
-    lo = (products - hi.astype(F32)).astype(BF)
-    flipped = jnp.dot(hi, flip, preferred_element_type=F32) + jnp.dot(lo, flip, preferred_element_type=F32)
-    rows = []
-    for g in range(products.shape[0] // 8):
-        one = pltpu.roll(flipped[8 * g : 8 * g + 8], 0, 1, stride=1, stride_axis=0)
-        rows.append(jnp.sum(one, axis=0, keepdims=True))
-    return jnp.concatenate(rows, axis=0)
+def lag_sums(products_ref, flip):
+    count = products_ref.shape[0] // 8
+    total = products_ref[pl.ds(0, count, stride=8), :]
+    for b in range(1, 8):
+        total = total + pltpu.roll(products_ref[pl.ds(b, count, stride=8), :], TAPS - b, 1)
+    hi = total.astype(BF)
+    lo = (total - hi.astype(F32)).astype(BF)
+    return jnp.dot(hi, flip, preferred_element_type=F32) + jnp.dot(lo, flip, preferred_element_type=F32)
 
 
 def taps_kernel(arr_ref, gate_ref, beh_ref, own_ref, mask_ref, s0_ref, s1_ref, g_ref, acc_ref):
@@ -45,7 +44,7 @@
             for a in range(1, 16):
                 part = part + pltpu.roll(both[8 * a : 8 * a + 8], 128 - 8 * a, 1)
             acc_ref[64 * h + 8 * g : 64 * h + 8 * g + 8, :] = part
-    sums = lag_sums(acc_ref[...], flip)
+    sums = lag_sums(acc_ref, flip)
     per = g_ref.shape[1]
     for i in range(g_ref.shape[0]):
         g_ref[i] = sums[per * i : per * i + per].astype(BF)

time: 82.4 us -> 83.1 us (level)
  transfers between devices with their start and end apart: 6 -> 6, of which waited for: 3 -> 3; matrix products, arithmetic and copies ran while one was open for 0% -> 0% of each run, Pallas kernels for 13% -> 12%
where the time goes in v3:
time: 83.1 us; the launch traced here: 82.7 us
  starting transfers between devices  39.4 us (47%)
  waiting for transfers between devices  22.9 us (28%)
  Pallas kernels  17.3 us (21%)
  local copies, waits for them, and re-layouts  2.45 us (3%)
    all_to_all x2, starting transfers between devices, exchanged(): return lax.all_to_all(value, 'ctx', 0, 0, axis_index_groups=groups)  26 us
    ppermute x4, starting transfers between devices, shifted(): return lax.ppermute(value, axis, pairs)  13.3 us
    ppermute x4, waiting for transfers between devices, shifted(): return lax.ppermute(value, axis, pairs)  12.8 us
    all_to_all x2, waiting for transfers between devices, exchanged(): return lax.all_to_all(value, 'ctx', 0, 0, axis_index_groups=groups)  10.1 us
    pallas_call x2, Pallas kernels, rows_block(): pl.pallas_call(functools.partial(rows_kernel, start, offset, width), in_s...  9.09 us
    pallas_call x1, Pallas kernels, taps_sums(): pl.pallas_call(taps_kernel, in_specs=[VMEM] * 5, out_specs=[VMEM] * 3, ou...  6.32 us
    unnamed x8, local copies, waits for them, and re-layouts  2.45 us
  transfers between devices with their start and end apart: 6, of which 3 were waited for; matrix products, arithmetic and copies ran while one was open for 0% of the time, Pallas kernels for 12%

profile of v3, /device:TPU:1, one launch (start us, length us, event | category | flops | bytes accessed | tf_op | source)
XLA Modules:
  0.0 82.7 jit_solution(15042411183314487777)
XLA Ops:
  0.6 5.2 %collective-permute-start = (bf16[128,4096]{1,0:T(8,128)(2,1)}, bf16[128,4096]{1,0:T(8,128)(2,1)S(1)}, u32[]{:S(2)}, u32[]{:S(2)}) collective-permute-start(bf16[128,4096]{1,0:T(8,128)(2,1)} %bitcast.13), channel_id=1, source_target_pairs={{0,384},{128,0},{256,128},{384,256},{1,385},{129,1},{257,129},{385... | collective-permute-start | bytes 3145736 | tf_op jit(solution)/shard_map/ppermute | solution.py:219
  5.9 4.0 %collective-permute-start.1 = (bf16[128,4096]{1,0:T(8,128)(2,1)}, bf16[128,4096]{1,0:T(8,128)(2,1)S(1)}, u32[]{:S(2)}, u32[]{:S(2)}) collective-permute-start(bf16[128,4096]{1,0:T(8,128)(2,1)} %bitcast.8), channel_id=1, source_target_pairs={{0,1},{1,2},{2,3},{3,4},{4,5},{5,6},{6,7},{7,8},{8,9},{9,10},{10,1... | collective-permute-start | bytes 3145736 | tf_op jit(solution)/shard_map/ppermute | solution.py:219
  9.9 0.0 copy-start
  9.9 1.2 %copy-done = bf16[1,128,4096]{2,1,0:T(8,128)(2,1)S(1)} copy-done((bf16[1,128,4096]{2,1,0:T(8,128)(2,1)S(1)}, bf16[1,128,4096]{2,1,0:T(8,128)(2,1)}, u32[]{:S(2)}) %copy-start) | copy-done | bytes 1048600
  11.1 0.0 copy-start.1
  11.1 1.2 %copy-done.1 = bf16[1,128,4096]{2,1,0:T(8,128)(2,1)S(1)} copy-done((bf16[1,128,4096]{2,1,0:T(8,128)(2,1)S(1)}, bf16[1,128,4096]{2,1,0:T(8,128)(2,1)}, u32[]{:S(2)}) %copy-start.1) | copy-done | bytes 1048600
  12.4 0.2 held.1
  12.5 0.0 copy-start.3
  12.5 12.8 %collective-permute-done.arr_ref = bf16[128,4096]{1,0:T(8,128)(2,1)S(1)} collective-permute-done((bf16[128,4096]{1,0:T(8,128)(2,1)}, bf16[128,4096]{1,0:T(8,128)(2,1)S(1)}, u32[]{:S(2)}, u32[]{:S(2)}) %collective-permute-start) | collective-permute-done | bytes 1048608 | tf_op jit(solution)/shard_map/ppermute | solution.py:219
  25.3 0.0 copy-done.3
  25.3 0.2 masks.1
  25.6 0.0 collective-permute-done.1.beh_ref
  25.6 6.3 %taps_sums.1 = (bf16[128,2048]{1,0:T(8,128)(2,1)S(1)}, bf16[128,2048]{1,0:T(8,128)(2,1)S(1)}, bf16[32,8,128]{2,1,0:T(8,128)(2,1)}) custom-call(bf16[128,4096]{1,0:T(8,128)(2,1)S(1)} %collective-permute-done.arr_ref, bf16[128,4096]{1,0:T(8,128)(2,1)S(1)} %get-tuple-element.11.gate_ref, bf16[128,4096]{1,0:T(8,128)(2,1)S(1)} %collective-permute-done.1.beh_ref, ...), custom_call_target="tpu_custom_call" | custom-call | flops 1073741824 | bytes 8388608 | tf_op jit(solution)/shard_map/taps_sums/pallas_call | solution.py:55
  31.9 13.3 %all-to-all-start = ((bf16[32,8,128]{2,1,0:T(8,128)(2,1)}), bf16[32,8,128]{2,1,0:T(8,128)(2,1)S(1)}, u32[]{:S(2)}, u32[]{:S(2)}) async-start(bf16[32,8,128]{2,1,0:T(8,128)(2,1)} %get-tuple-element.18), calls=%async_computation | async-start | bytes 131072 | tf_op jit(solution)/shard_map/all_to_all | solution.py:223
  45.2 2.1 %collective-permute-start.2 = (bf16[128,2048]{1,0:T(8,128)(2,1)S(1)}, bf16[128,2048]{1,0:T(8,128)(2,1)S(1)}, u32[]{:S(2)}, u32[]{:S(2)}) collective-permute-start(bf16[128,2048]{1,0:T(8,128)(2,1)S(1)} %get-tuple-element.15.s_ref), channel_id=1, source_target_pairs={{1,0},{2,1},{3,2},{4,3},{5,4},{6,5},{7,6},{8,7},{9,8},{10,9},{11,1... | collective-permute-start | bytes 1572872 | tf_op jit(solution)/shard_map/ppermute | solution.py:219
  47.3 1.9 %collective-permute-start.3 = (bf16[128,2048]{1,0:T(8,128)(2,1)S(1)}, bf16[128,2048]{1,0:T(8,128)(2,1)S(1)}, u32[]{:S(2)}, u32[]{:S(2)}) collective-permute-start(bf16[128,2048]{1,0:T(8,128)(2,1)S(1)} %get-tuple-element.17.s_ref), channel_id=1, source_target_pairs={{1,0},{2,1},{3,2},{4,3},{5,4},{6,5},{7,6},{8,7},{9,8},{10,9},{11,1... | collective-permute-start | bytes 1572872 | tf_op jit(solution)/shard_map/ppermute | solution.py:219
  49.3 4.0 %all-to-all-done.parts_ref = bf16[32,8,128]{2,1,0:T(8,128)(2,1)S(1)} async-done(((bf16[32,8,128]{2,1,0:T(8,128)(2,1)}), bf16[32,8,128]{2,1,0:T(8,128)(2,1)S(1)}, u32[]{:S(2)}, u32[]{:S(2)}) %all-to-all-start) | async-done | bytes 65568 | tf_op jit(solution)/shard_map/all_to_all | solution.py:223
  53.2 0.8 sum_of_32.1
  54.0 0.0 copy-start.2
  54.0 12.7 %all-to-all-start.1 = ((bf16[128,8,128]{2,1,0:T(8,128)(2,1)}), bf16[128,8,128]{2,1,0:T(8,128)(2,1)S(1)}, u32[]{:S(2)}, u32[]{:S(2)}) async-start(bf16[128,8,128]{2,1,0:T(8,128)(2,1)} %sum_of_32.1), calls=%async_computation.1 | async-start | bytes 524288 | tf_op jit(solution)/shard_map/all_to_all | solution.py:223
  66.8 0.0 collective-permute-done.3.ahead_ref
  66.8 0.0 copy-done.2
  66.8 4.5 %rows_block_0.1.rest_0_ = bf16[128,4096]{1,0:T(8,128)(2,1)} custom-call(bf16[128,2048]{1,0:T(8,128)(2,1)S(1)} %get-tuple-element.17.s_ref, bf16[128,2048]{1,0:T(8,128)(2,1)S(1)} %collective-permute-done.3.ahead_ref, f32[256,128]{1,0:T(8,128)S(1)} %bitcast.10, bf16[128,256]{1,0:T(8,128)(2,1)S(1)} %get-tuple-element.16.mask_ref), custom_call_target="tpu_custom_call" | custom-call | flops 34359738368 | bytes 2097152 | tf_op jit(solution)/shard_map/rows_block_0/pallas_call | solution.py:96
  71.3 0.0 collective-permute-done.2.ahead_ref
  71.3 4.5 %rows_block_2048.1 = bf16[128,4096]{1,0:T(8,128)(2,1)} custom-call(bf16[128,2048]{1,0:T(8,128)(2,1)S(1)} %get-tuple-element.15.s_ref, bf16[128,2048]{1,0:T(8,128)(2,1)S(1)} %collective-permute-done.2.ahead_ref, f32[256,128]{1,0:T(8,128)S(1)} %bitcast.11, bf16[128,256]{1,0:T(8,128)(2,1)S(1)} %get-tuple-element.16.mask_ref, ...), custom_call_target="tpu_custom_call", output_to_operand_aliasing={{}: (4, {})} | custom-call | flops 34359738368 | bytes 2097152 | tf_op jit(solution)/shard_map/rows_block_2048/pallas_call | solution.py:96
  75.9 6.1 %all-to-all-done.1.parts_ref = bf16[128,8,128]{2,1,0:T(8,128)(2,1)S(1)} async-done(((bf16[128,8,128]{2,1,0:T(8,128)(2,1)}), bf16[128,8,128]{2,1,0:T(8,128)(2,1)S(1)}, u32[]{:S(2)}, u32[]{:S(2)}) %all-to-all-start.1) | async-done | bytes 262176 | tf_op jit(solution)/shard_map/all_to_all | solution.py:223
  82.0 0.7 last_sum.1
Async XLA Ops:
  0.6 24.7 %collective-permute-start = (bf16[128,4096]{1,0:T(8,128)(2,1)}, bf16[128,4096]{1,0:T(8,128)(2,1)S(1)}, u32[]{:S(2)}, u32[]{:S(2)}) collective-permute-start(bf16[128,4096]{1,0:T(8,128)(2,1)} %bitcast.13), channel_id=1, source_target_pairs={{0,384},{128,0},{256,128},{384,256},{1,385},{129,1},{257,129},{385... | collective-permute-start | bytes 3145736 | tf_op jit(solution)/shard_map/ppermute | solution.py:219
  5.9 19.7 %collective-permute-start.1 = (bf16[128,4096]{1,0:T(8,128)(2,1)}, bf16[128,4096]{1,0:T(8,128)(2,1)S(1)}, u32[]{:S(2)}, u32[]{:S(2)}) collective-permute-start(bf16[128,4096]{1,0:T(8,128)(2,1)} %bitcast.8), channel_id=1, source_target_pairs={{0,1},{1,2},{2,3},{3,4},{4,5},{5,6},{6,7},{7,8},{8,9},{9,10},{10,1... | collective-permute-start | bytes 3145736 | tf_op jit(solution)/shard_map/ppermute | solution.py:219
  9.9 1.2 %copy-start = (bf16[1,128,4096]{2,1,0:T(8,128)(2,1)S(1)}, bf16[1,128,4096]{2,1,0:T(8,128)(2,1)}, u32[]{:S(2)}) copy-start(bf16[1,128,4096]{2,1,0:T(8,128)(2,1)} %param.5) | copy-start | bytes 3145732
  11.1 1.2 %copy-start.1 = (bf16[1,128,4096]{2,1,0:T(8,128)(2,1)S(1)}, bf16[1,128,4096]{2,1,0:T(8,128)(2,1)}, u32[]{:S(2)}) copy-start(bf16[1,128,4096]{2,1,0:T(8,128)(2,1)} %param.6) | copy-start | bytes 3145732
  12.5 12.8 %copy-start.3 = (s32[1,128]{1,0:T(1,128)S(1)}, s32[1,128]{1,0:T(1,128)}, u32[]{:S(2)}) copy-start(s32[1,128]{1,0:T(1,128)} %len_ref) | copy-start | bytes 1540
  31.9 21.4 %all-to-all-start = ((bf16[32,8,128]{2,1,0:T(8,128)(2,1)}), bf16[32,8,128]{2,1,0:T(8,128)(2,1)S(1)}, u32[]{:S(2)}, u32[]{:S(2)}) async-start(bf16[32,8,128]{2,1,0:T(8,128)(2,1)} %get-tuple-element.18), calls=%async_computation | async-start | bytes 131072 | tf_op jit(solution)/shard_map/all_to_all | solution.py:223
  45.2 26.2 %collective-permute-start.2 = (bf16[128,2048]{1,0:T(8,128)(2,1)S(1)}, bf16[128,2048]{1,0:T(8,128)(2,1)S(1)}, u32[]{:S(2)}, u32[]{:S(2)}) collective-permute-start(bf16[128,2048]{1,0:T(8,128)(2,1)S(1)} %get-tuple-element.15.s_ref), channel_id=1, source_target_pairs={{1,0},{2,1},{3,2},{4,3},{5,4},{6,5},{7,6},{8,7},{9,8},{10,9},{11,1... | collective-permute-start | bytes 1572872 | tf_op jit(solution)/shard_map/ppermute | solution.py:219
  47.3 19.4 %collective-permute-start.3 = (bf16[128,2048]{1,0:T(8,128)(2,1)S(1)}, bf16[128,2048]{1,0:T(8,128)(2,1)S(1)}, u32[]{:S(2)}, u32[]{:S(2)}) collective-permute-start(bf16[128,2048]{1,0:T(8,128)(2,1)S(1)} %get-tuple-element.17.s_ref), channel_id=1, source_target_pairs={{1,0},{2,1},{3,2},{4,3},{5,4},{6,5},{7,6},{8,7},{9,8},{10,9},{11,1... | collective-permute-start | bytes 1572872 | tf_op jit(solution)/shard_map/ppermute | solution.py:219
  54.0 12.8 %copy-start.2 = (f32[1,256,128]{2,1,0:T(8,128)S(1)}, f32[1,256,128]{2,1,0:T(8,128)}, u32[]{:S(2)}) copy-start(f32[1,256,128]{2,1,0:T(8,128)} %param.8) | copy-start | bytes 393220
  54.0 28.0 %all-to-all-start.1 = ((bf16[128,8,128]{2,1,0:T(8,128)(2,1)}), bf16[128,8,128]{2,1,0:T(8,128)(2,1)S(1)}, u32[]{:S(2)}, u32[]{:S(2)}) async-start(bf16[128,8,128]{2,1,0:T(8,128)(2,1)} %sum_of_32.1), calls=%async_computation.1 | async-start | bytes 524288 | tf_op jit(solution)/shard_map/all_to_all | solution.py:223
